TPU v7x, 32 devices: a whole 2x2x4 slice. The times are simulated.
32 devices in a mesh: expert: 8 (over y, x, core), tensor: 4 (over z).
Axes of the slice: x: 2, y: 2, z: 4, core: 2. Of those that a mesh axis runs over, the one named last changes fastest.
Arguments:
- tokens: bfloat16 [1024, 7168], P(('expert', 'tensor')), may hold values from -54 to 54
- dense_in: bfloat16 [2, 2432, 7168], P(None, 'tensor'), may hold values from -1 to 1
- dense_out: bfloat16 [2432, 7168], P('tensor'), may hold values from -1 to 1
- expert_in: bfloat16 [8, 2, 2432, 7168], P('expert', None, 'tensor'), may hold values from -1 to 1
- expert_out: bfloat16 [8, 2432, 7168], P('expert', 'tensor'), may hold values from -1 to 1
- norm_gains: float32 [3, 7168], replicated, may hold values from 0 to 2
- expert_ids: int32 [1024, 2], P('expert'), may hold values from 0 to 7, as said below
- gate_probs: float32 [1024, 2], P('expert'), may hold values from 0 to 1
- cotangent: bfloat16 [1024, 7168], P(('expert', 'tensor')), may hold values from -6 to 6
Outputs:
- layer_output: bfloat16 [1024, 7168], P(('expert', 'tensor'))
- input_grad: bfloat16 [1024, 7168], P(('expert', 'tensor'))
Inputs may be any that keep to these rules, and one draw needn't show every extreme that they name: `expert_ids`: the ids of one row differ; in each aligned block of 128 rows (the tokens of one index of expert) no id stands in more than 48 rows, and some id in exactly 48; every id stands in every block.
All inputs are finite; a program needn't handle non-finite values.
Results may differ from a plain program's by a relative error of at most 0.028.
Values may be sent and summed in bfloat16 or wider, within the bound.
A program may use at most 128 MiB of HBM per device.

v0:
```python
import jax
import jax.numpy as jnp
from jax import lax
from jax.sharding import PartitionSpec as P

epsilon = 1e-05


def rms_scale(values):
    return lax.rsqrt(jnp.mean(values * values, axis=-1, keepdims=True) + epsilon)


def norm_grad(values, gain_row, upstream):
    factor = rms_scale(values)
    weighted = gain_row * upstream
    inner_mean = jnp.mean(weighted * values, axis=-1, keepdims=True)
    return factor * weighted - values * factor * factor * factor * inner_mean


def silu_grad(preact):
    sigmoid_value = jax.nn.sigmoid(preact)
    return sigmoid_value * (1.0 + preact * (1.0 - sigmoid_value))


def slot_table(group_ids, experts, capacity):
    routes = group_ids.reshape(-1)
    route_total = routes.shape[0]
    onehot = (routes[:, None] == jnp.arange(experts, dtype=jnp.int32)[None, :]).astype(jnp.int32)
    earlier = jnp.cumsum(onehot, axis=0) - onehot
    slot_index = jnp.sum(earlier * onehot, axis=1)
    position = routes * capacity + slot_index
    inverse = jnp.full((experts * capacity,), route_total, jnp.int32)
    inverse = inverse.at[position].set(jnp.arange(route_total, dtype=jnp.int32))
    return (position, inverse)


def per_device(
    tokens,
    dense_in,
    dense_out,
    expert_in,
    expert_out,
    norm_gains,
    expert_ids,
    gate_probs,
    cotangent,
):
    experts = lax.axis_size("expert") * expert_in.shape[0]
    group_rows = expert_ids.shape[0]
    top_count = expert_ids.shape[1]
    capacity = 3 * group_rows * top_count // (2 * experts)
    model_width = tokens.shape[1]
    weight_in = expert_in[0]
    weight_out = expert_out[0]
    source = tokens.astype(jnp.float32)
    normed_local = (source * rms_scale(source) * norm_gains[0]).astype(jnp.bfloat16)
    normed = lax.all_gather(normed_local, "tensor", axis=0, tiled=True)
    preact_dense = jnp.einsum("gd,khd->gkh", normed, dense_in, preferred_element_type=jnp.float32)
    hidden_dense = (jax.nn.silu(preact_dense[:, 0]) * preact_dense[:, 1]).astype(jnp.bfloat16)
    dense_part = jnp.dot(hidden_dense, dense_out, preferred_element_type=jnp.float32)
    position, inverse = slot_table(expert_ids, experts, capacity)
    padded = jnp.concatenate([normed, jnp.zeros((1, model_width), jnp.bfloat16)], axis=0)
    buffer = jnp.take(padded, inverse // top_count, axis=0).reshape(experts, capacity, model_width)
    preact = jnp.einsum(
        "scd,khd->sckh",
        lax.all_to_all(buffer, "expert", split_axis=0, concat_axis=0, tiled=True),
        weight_in,
        preferred_element_type=jnp.float32,
    )
    hidden = (jax.nn.silu(preact[:, :, 0]) * preact[:, :, 1]).astype(jnp.bfloat16)
    partial_value = jnp.einsum(
        "sch,hd->scd", hidden, weight_out, preferred_element_type=jnp.float32
    )
    partial_value, preact_expert = (partial_value.astype(jnp.bfloat16), preact)
    returned = lax.all_to_all(partial_value, "expert", split_axis=0, concat_axis=0, tiled=True)
    flat_rows = jnp.take(returned.reshape(experts * capacity, model_width), position, axis=0)
    flat_rows = flat_rows.reshape(group_rows, top_count, model_width)
    mixture_part = jnp.sum(flat_rows.astype(jnp.float32) * gate_probs[:, :, None], axis=1)
    dense_raw, mixture_raw = (
        lax.psum_scatter(
            dense_part.astype(jnp.bfloat16), "tensor", scatter_dimension=0, tiled=True
        ).astype(jnp.float32),
        lax.psum_scatter(
            mixture_part.astype(jnp.bfloat16), "tensor", scatter_dimension=0, tiled=True
        ).astype(jnp.float32),
    )
    layer_output = (
        source
        + dense_raw * rms_scale(dense_raw) * norm_gains[1]
        + mixture_raw * rms_scale(mixture_raw) * norm_gains[2]
    ).astype(jnp.bfloat16)
    upstream = cotangent.astype(jnp.float32)
    dense_grad = norm_grad(dense_raw, norm_gains[1], upstream).astype(jnp.bfloat16)
    mixture_grad = norm_grad(mixture_raw, norm_gains[2], upstream).astype(jnp.bfloat16)
    dense_rows, mixture_rows = (
        lax.all_gather(dense_grad, "tensor", axis=0, tiled=True),
        lax.all_gather(mixture_grad, "tensor", axis=0, tiled=True),
    )
    back_dense = jnp.einsum("gd,hd->gh", dense_rows, dense_out, preferred_element_type=jnp.float32)
    gate_dense = (back_dense * preact_dense[:, 1] * silu_grad(preact_dense[:, 0])).astype(
        jnp.bfloat16
    )
    up_dense = (back_dense * jax.nn.silu(preact_dense[:, 0])).astype(jnp.bfloat16)
    dense_input = jnp.dot(gate_dense, dense_in[0], preferred_element_type=jnp.float32) + jnp.dot(
        up_dense, dense_in[1], preferred_element_type=jnp.float32
    )
    scaled = (gate_probs[:, :, None] * mixture_rows[:, None, :].astype(jnp.float32)).astype(
        jnp.bfloat16
    )
    scaled = scaled.reshape(group_rows * top_count, model_width)
    padded_grad = jnp.concatenate([scaled, jnp.zeros((1, model_width), jnp.bfloat16)], axis=0)
    grad_buffer = jnp.take(padded_grad, inverse, axis=0).reshape(experts, capacity, model_width)
    back_expert = jnp.einsum(
        "scd,hd->sch",
        lax.all_to_all(grad_buffer, "expert", split_axis=0, concat_axis=0, tiled=True),
        weight_out,
        preferred_element_type=jnp.float32,
    )
    gate_expert = (back_expert * preact_expert[:, :, 1] * silu_grad(preact_expert[:, :, 0])).astype(
        jnp.bfloat16
    )
    up_expert = (back_expert * jax.nn.silu(preact_expert[:, :, 0])).astype(jnp.bfloat16)
    input_part = (
        jnp.einsum("sch,hd->scd", gate_expert, weight_in[0], preferred_element_type=jnp.float32)
        + jnp.einsum("sch,hd->scd", up_expert, weight_in[1], preferred_element_type=jnp.float32)
    ).astype(jnp.bfloat16)
    returned_grad = lax.all_to_all(input_part, "expert", split_axis=0, concat_axis=0, tiled=True)
    grad_rows = jnp.take(returned_grad.reshape(experts * capacity, model_width), position, axis=0)
    mixture_input = jnp.sum(
        grad_rows.reshape(group_rows, top_count, model_width).astype(jnp.float32), axis=1
    )
    input_total = lax.psum_scatter(
        (dense_input + mixture_input).astype(jnp.bfloat16),
        "tensor",
        scatter_dimension=0,
        tiled=True,
    ).astype(jnp.float32)
    input_grad = norm_grad(source, norm_gains[0], input_total).astype(jnp.bfloat16)
    return (layer_output, input_grad)


def solution(mesh):
    placed = (
        P(("expert", "tensor"), None),
        P(None, "tensor", None),
        P("tensor", None),
        P("expert", None, "tensor", None),
        P("expert", "tensor", None),
        P(),
        P("expert", None),
        P("expert", None),
        P(("expert", "tensor"), None),
    )
    return jax.shard_map(
        per_device,
        mesh=mesh,
        in_specs=placed,
        out_specs=(P(("expert", "tensor"), None), P(("expert", "tensor"), None)),
        check_vma=False,
    )
```

profile of v0, /device:TPU:0, one launch (start us, length us, event | category | flops | bytes accessed | tf_op | source)
XLA Modules:
  0.0 644.5 jit_solution(1805136784948187260)
XLA Ops:
  16.7 39.8 %all-gather.4.cloned.1.call-done = bf16[128,7168]{1,0:T(8,128)(2,1)} async-done(((bf16[32,7168]{1,0:T(8,128)(2,1)}), bf16[128,7168]{1,0:T(8,128)(2,1)}) %all-gather.4.cloned.1.call-update) | async-done | bytes 1835024 | tf_op jit(solution)/shard_map/all_gather | solution.py:57
  58.1 6.5 %gather_fusion = bf16[384,7168]{1,0:T(8,128)(2,1)} fusion(bf16[129,7168]{1,0:T(8,128)(2,1)S(1)} %concatenate.6, s32[1024]{0:T(1024)S(1)} %pad_clamp_fusion.2), kind=kCustom, calls=%fused_computation.2 | custom fusion | bytes 11011584 | tf_op jit(solution)/shard_map/jit(_take)/gather | solution.py:63
  67.8 66.6 %all_to_all.20 = bf16[8,48,7168]{2,1,0:T(8,128)(2,1)S(1)} all-to-all(bf16[8,48,7168]{2,1,0:T(8,128)(2,1)S(1)} %broadcast_select_fusion.1), channel_id=1, replica_groups=mesh['expert'=8,'tensor'=4] {'expert'}, dimensions={0} | all-to-all | bytes 11010048 | tf_op jit(solution)/shard_map/all_to_all | solution.py:66
  134.3 12.4 %fusion = f32[8,48,2,608]{3,1,2,0:T(8,128)S(1)} fusion(bf16[1,2,608,7168]{3,2,1,0:T(8,128)(2,1)} %param.14, bf16[8,48,7168]{2,1,0:T(8,128)(2,1)S(1)} %all_to_all.20), kind=kOutput, calls=%fused_computation.5 | convolution fusion | flops 6694109184 | bytes 24805376 | tf_op jit(solution)/shard_map/scd,khd->sckh/dot_general | solution.py:64
  148.0 9.8 %convolution_convert_fusion = bf16[8,48,7168]{2,1,0:T(8,128)(2,1)} fusion(bf16[1,608,7168]{2,1,0:T(8,128)(2,1)} %param.15, f32[8,48,2,608]{3,1,2,0:T(8,128)S(1)} %fusion), kind=kOutput, calls=%fused_computation.8 | convolution fusion | flops 3351207936 | bytes 16089088 | tf_op jit(solution)/shard_map/sch,hd->scd/dot_general | solution.py:71
  157.8 4.8 all-to-all-start.1
  162.9 8.4 %fusion.26 = f32[128,2,608]{0,2,1:T(8,128)S(1)} fusion(bf16[2,608,7168]{2,1,0:T(8,128)(2,1)} %param.12, bf16[128,7168]{1,0:T(8,128)(2,1)S(1)} %copy-done.1), kind=kOutput, calls=%fused_computation.34 | convolution fusion | flops 2231369728 | bytes 19890176 | tf_op jit(solution)/shard_map/gd,khd->gkh/dot_general | solution.py:58
  171.3 6.4 convolution_convert_fusion.1
  177.9 47.9 %all-to-all-done.1 = bf16[8,48,7168]{2,1,0:T(8,128)(2,1)} async-done(((bf16[8,48,7168]{2,1,0:T(8,128)(2,1)}), bf16[8,48,7168]{2,1,0:T(8,128)(2,1)}, u32[]{:S(2)}, u32[]{:S(2)}) %all-to-all-start.1) | async-done | bytes 5505056 | tf_op jit(solution)/shard_map/all_to_all | solution.py:75
  225.8 11.4 %gather_fusion.2 = bf16[256,7168]{1,0:T(8,128)(2,1)} fusion(bf16[384,7168]{1,0:T(8,128)(2,1)} %bitcast.18, s32[1024]{0:T(1024)S(1)} %pad_clamp_fusion.1), kind=kCustom, calls=%fused_computation.clone | custom fusion | bytes 7341056 | tf_op jit(solution)/shard_map/jit(_take)/gather | solution.py:76
  237.2 5.6 select_convert_fusion.1
  242.8 9.3 %reshape.141 = f32[128,2,7168]{2,1,0:T(2,128)} reshape(f32[256,7168]{1,0:T(8,128)} %select_convert_fusion.1) | data formatting | bytes 14680064 | tf_op jit(solution)/shard_map/convert_element_type | solution.py:78
  252.0 12.4 %multiply_reduce_fusion = bf16[128,7168]{1,0:T(8,128)(2,1)} fusion(f32[128,2,7168]{2,1,0:T(2,128)} %reshape.141, f32[128,2]{1,0:T(8,128)S(1)} %copy.19), kind=kLoop, calls=%fused_computation.28 | loop fusion | flops 2752512 | bytes 9176064 | tf_op jit(solution)/shard_map/reduce_sum | solution.py:78
  264.8 36.4 %reduce-scatter.6.cloned.1.call-done = bf16[32,7168]{1,0:T(8,128)(2,1)} async-done(((bf16[128,7168]{1,0:T(8,128)(2,1)}), bf16[32,7168]{1,0:T(8,128)(2,1)}) %reduce-scatter.6.cloned.1.call-update) | async-done | bytes 458768 | tf_op jit(solution)/shard_map/reduce_scatter | solution.py:83
  306.0 40.4 %all-gather.8.cloned.1.call-done = bf16[128,7168]{1,0:T(8,128)(2,1)} async-done(((bf16[32,7168]{1,0:T(8,128)(2,1)}), bf16[128,7168]{1,0:T(8,128)(2,1)}) %all-gather.8.cloned.1.call-update) | async-done | bytes 1835024 | tf_op jit(solution)/shard_map/all_gather | solution.py:97
  346.4 6.8 %mul.333 = f32[128,2,7168]{2,1,0:T(2,128)} broadcast(bf16[128,7168]{1,0:T(8,128)(2,1)} %all-gather.8.cloned.1.call-done), dimensions={0,2} | broadcast | bytes 9175040 | tf_op jit(solution)/shard_map/mul | solution.py:107
  353.2 9.5 %mul.334 = f32[256,7168]{1,0:T(8,128)} reshape(f32[128,2,7168]{2,1,0:T(2,128)} %mul.333) | data formatting | bytes 14680064 | tf_op jit(solution)/shard_map/mul | solution.py:107
  369.0 15.8 %gather_fusion.1 = bf16[384,7168]{1,0:T(8,128)(2,1)} fusion(bf16[257,7168]{1,0:T(8,128)(2,1)} %concatenate.7, s32[1024]{0:T(1024)S(1)} %pad_clamp_fusion), kind=kCustom, calls=%fused_computation.3 | custom fusion | bytes 11011584 | tf_op jit(solution)/shard_map/jit(_take)/gather | solution.py:112
  388.1 67.2 %all_to_all.21 = bf16[8,48,7168]{2,1,0:T(8,128)(2,1)S(1)} all-to-all(bf16[8,48,7168]{2,1,0:T(8,128)(2,1)S(1)} %broadcast_select_fusion), channel_id=1, replica_groups=mesh['expert'=8,'tensor'=4] {'expert'}, dimensions={0} | all-to-all | bytes 11010048 | tf_op jit(solution)/shard_map/all_to_all | solution.py:115
  459.8 10.9 %fusion.3 = f32[8,48,7168]{2,1,0:T(8,128)} fusion(bf16[1,2,608,7168]{3,2,1,0:T(8,128)(2,1)} %param.14, f32[8,48,608]{2,1,0:T(8,128)S(1)} %fusion.9, f32[8,48,2,608]{3,1,2,0:T(8,128)S(1)} %copy-done.9), kind=kOutput, calls=%fused_computation.10 | convolution fusion | flops 3349389312 | bytes 22528000 | tf_op jit(solution)/shard_map/sch,hd->scd/dot_general | solution.py:124
  470.7 11.3 %add_convert_fusion = bf16[8,48,7168]{2,1,0:T(8,128)(2,1)} fusion(f32[8,48,7168]{2,1,0:T(8,128)} %fusion.3, bf16[1,2,608,7168]{3,2,1,0:T(8,128)(2,1)} %param.14, f32[8,48,608]{2,1,0:T(8,128)S(1)} %fusion.9, f32[8,48,2,608]{3,1,2,0:T(8,128)S(1)} %copy-done.10), kind=kOutput, calls=%fused_computation.7 | convolution fusion | flops 3353960448 | bytes 27197440 | tf_op jit(solution)/shard_map/sch,hd->scd/dot_general | solution.py:125
  482.1 4.7 all-to-all-start.3
  487.6 42.6 %all-gather.6.cloned.1.call-done = bf16[128,7168]{1,0:T(8,128)(2,1)} async-done(((bf16[32,7168]{1,0:T(8,128)(2,1)}), bf16[128,7168]{1,0:T(8,128)(2,1)}) %all-gather.6.cloned.1.call-update) | async-done | bytes 1835024 | tf_op jit(solution)/shard_map/all_gather | solution.py:96
  530.2 6.4 fusion.95
  536.6 7.0 %fusion.5 = f32[128,7168]{1,0:T(8,128)} fusion(bf16[2,608,7168]{2,1,0:T(8,128)(2,1)} %param.12, f32[128,608]{0,1:T(8,128)S(1)} %fusion.95, f32[128,2,608]{0,2,1:T(8,128)S(1)} %fusion.26), kind=kOutput, calls=%fused_computation.12 | convolution fusion | flops 1116151808 | bytes 13008896 | tf_op jit(solution)/shard_map/dot_general | solution.py:104
  543.6 6.3 all-to-all-done.3
  549.9 11.4 %gather_fusion.3 = bf16[256,7168]{1,0:T(8,128)(2,1)} fusion(bf16[384,7168]{1,0:T(8,128)(2,1)} %bitcast.29, s32[1024]{0:T(1024)S(1)} %pad_clamp_fusion.1), kind=kCustom, calls=%fused_computation.1.clone | custom fusion | bytes 7341056 | tf_op jit(solution)/shard_map/jit(_take)/gather | solution.py:128
  561.3 5.6 select_convert_fusion
  566.8 9.5 %reshape.142 = f32[128,2,7168]{2,1,0:T(2,128)} reshape(f32[256,7168]{1,0:T(8,128)} %select_convert_fusion) | data formatting | bytes 14680064 | tf_op jit(solution)/shard_map/convert_element_type | solution.py:130
  576.3 12.3 %reduce_sum.103 = f32[128,7168]{1,0:T(8,128)} reduce(f32[128,2,7168]{2,1,0:T(2,128)} %reshape.142, f32[]{:T(128)} %constant.72.clone.1), dimensions={1}, to_apply=%region_12.14 | reduce | flops 917504 | bytes 11010052 | tf_op jit(solution)/shard_map/reduce_sum | solution.py:129
  588.6 8.8 %fusion.22 = bf16[128,7168]{1,0:T(8,128)(2,1)} fusion(f32[128,7168]{1,0:T(8,128)} %reduce_sum.103, f32[128,7168]{1,0:T(8,128)} %fusion.5, bf16[2,608,7168]{2,1,0:T(8,128)(2,1)} %param.12, f32[128,608]{0,1:T(8,128)S(1)} %fusion.95, f32[128,2,608]{0,2,1:T(8,128)S(1)} %fusion.26), kind=kOutput, calls=%fused_computation.25 | convolution fusion | flops 1119215616 | bytes 18825216 | tf_op jit(solution)/shard_map/dot_general | solution.py:104
  597.4 36.7 %reduce-scatter.8.cloned.1.call-done = bf16[32,7168]{1,0:T(8,128)(2,1)} async-done(((bf16[128,7168]{1,0:T(8,128)(2,1)}), bf16[32,7168]{1,0:T(8,128)(2,1)}) %reduce-scatter.8.cloned.1.call-update) | async-done | bytes 458768 | tf_op jit(solution)/shard_map/reduce_scatter | solution.py:132
  (84 shorter events, 39.2 us)
Async XLA Ops:
  7.2 49.3 %all-gather.4.cloned.1.call-start = ((), (), s32[]{:S(2)}) async-start(), calls=%async_computation.7 | async-start | bytes 2293760 | tf_op jit(solution)/shard_map/all_gather | solution.py:57
  8.3 1.3 copy-start.3
  9.6 0.6 copy-start.5
  146.8 1.3 copy-start.8
  157.8 5.0 copy-start.1
  157.8 68.0 %all-to-all-start.1 = ((bf16[8,48,7168]{2,1,0:T(8,128)(2,1)}), bf16[8,48,7168]{2,1,0:T(8,128)(2,1)}, u32[]{:S(2)}, u32[]{:S(2)}) async-start(bf16[8,48,7168]{2,1,0:T(8,128)(2,1)} %convolution_convert_fusion), calls=%async_computation.2 | async-start | bytes 11010048 | tf_op jit(solution)/shard_map/all_to_all | solution.py:75
  162.7 102.1 %reduce-scatter.4.cloned.1.call-start = ((), (), s32[]{:S(2)}) async-start(), calls=%async_computation.8 | async-start | bytes 2293760 | tf_op jit(solution)/shard_map/reduce_scatter | solution.py:80
  171.3 6.5 %copy-start.7 = (f32[128,2]{0,1:T(2,128)S(1)}, f32[128,2]{0,1:T(2,128)}, u32[]{:S(2)}) copy-start(f32[128,2]{0,1:T(2,128)} %param.18) | copy-start | bytes 3076
  177.8 123.4 %reduce-scatter.6.cloned.1.call-start = ((), (), s32[]{:S(2)}) async-start(), calls=%async_computation.9 | async-start | bytes 2293760 | tf_op jit(solution)/shard_map/reduce_scatter | solution.py:83
  252.0 49.1 %copy-start.2 = (bf16[32,7168]{1,0:T(8,128)(2,1)S(1)}, bf16[32,7168]{1,0:T(8,128)(2,1)}, u32[]{:S(2)}) copy-start(bf16[32,7168]{1,0:T(8,128)(2,1)} %param.19) | copy-start | bytes 1376260
  252.0 50.8 %copy-start = (bf16[32,7168]{1,0:T(8,128)(2,1)S(1)}, bf16[32,7168]{1,0:T(8,128)(2,1)}, u32[]{:S(2)}) copy-start(bf16[32,7168]{1,0:T(8,128)(2,1)} %param.11) | copy-start | bytes 1376260
  264.5 81.9 %all-gather.8.cloned.1.call-start = ((), (), s32[]{:S(2)}) async-start(), calls=%async_computation.11 | async-start | bytes 2293760 | tf_op jit(solution)/shard_map/all_gather | solution.py:97
  384.7 70.6 %slice-start = ((s8[8716288]{0:T(1024)(128)(4,1)}), s8[4194304]{0:T(1024)(128)(4,1)S(1)}, s32[]{:S(2)}) async-start(s8[8716288]{0:T(1024)(128)(4,1)} %bitcast.156), calls=%async_computation.13 | async-start | bytes 8388608
  384.7 70.6 %slice-start.1 = ((s8[8716288]{0:T(1024)(128)(4,1)}), s8[4194304]{0:T(1024)(128)(4,1)S(1)}, s32[]{:S(2)}) async-start(s8[8716288]{0:T(1024)(128)(4,1)} %bitcast.156), calls=%async_computation.14 | async-start | bytes 8388608
  388.0 67.3 %slice-start.2 = ((s8[8716288]{0:T(1024)(128)(4,1)}), s8[327680]{0:T(1024)(128)(4,1)S(1)}, s32[]{:S(2)}) async-start(s8[8716288]{0:T(1024)(128)(4,1)} %bitcast.156), calls=%async_computation.15 | async-start | bytes 655360
  455.3 4.5 copy-start.9
  459.8 10.9 %copy-start.10 = (f32[8,48,2,608]{3,1,2,0:T(8,128)S(1)}, f32[8,48,2,608]{3,1,2,0:T(8,128)}, u32[]{:S(2)}) copy-start(f32[8,48,2,608]{3,1,2,0:T(8,128)} %copy-done.8) | copy-start | bytes 5603332
  482.1 67.9 %all-to-all-start.3 = ((bf16[8,48,7168]{2,1,0:T(8,128)(2,1)}), bf16[8,48,7168]{2,1,0:T(8,128)(2,1)}, u32[]{:S(2)}, u32[]{:S(2)}) async-start(bf16[8,48,7168]{2,1,0:T(8,128)(2,1)} %add_convert_fusion), calls=%async_computation.5 | async-start | bytes 11010048 | tf_op jit(solution)/shard_map/all_to_all | solution.py:127
  486.7 43.4 %all-gather.6.cloned.1.call-start = ((), (), s32[]{:S(2)}) async-start(), calls=%async_computation.10 | async-start | bytes 2293760 | tf_op jit(solution)/shard_map/all_gather | solution.py:96
  487.3 146.7 %reduce-scatter.8.cloned.1.call-start = ((), (), s32[]{:S(2)}) async-start(), calls=%async_computation.12 | async-start | bytes 2293760 | tf_op jit(solution)/shard_map/reduce_scatter | solution.py:132
  588.6 45.5 %copy-start.4 = (f32[1,7168]{1,0:T(1,128)S(1)}, f32[1,7168]{1,0:T(1,128)}, u32[]{:S(2)}) copy-start(f32[1,7168]{1,0:T(1,128)} %copy-done.3) | copy-start | bytes 86020
  588.6 46.7 %copy-start.6 = (f32[32]{0:T(128)S(1)}, f32[32]{0:T(128)}, u32[]{:S(2)}) copy-start(f32[32]{0:T(128)} %copy-done.5) | copy-start | bytes 388
Sparse Core Ops, SparseCore 0:
  12.3 44.1 all-gather.3
  177.9 38.6 reduce-scatter.3
  264.6 36.4 reduce-scatter.5
  305.9 40.5 all-gather.7
  489.4 40.6 all-gather.5
  597.5 36.4 reduce-scatter.7
where the time goes:
time: 654 us; the launch traced here: 645 us
  waiting for transfers between devices  251 us (38%)
  blocking collectives  134 us (20%)
  local copies, waits for them, and re-layouts  90.4 us (14%)
  matrix products  85.9 us (13%)
  other arithmetic  58.7 us (9%)
  between operations  14.6 us (2%)
  starting transfers between devices  10.3 us (2%)
    all_to_all x1, blocking collectives, per_device(): lax.all_to_all(grad_buffer, 'expert', split_axis=0, concat_axis=0, tiled=...  67.2 us
    all_to_all x1, blocking collectives, per_device(): lax.all_to_all(buffer, 'expert', split_axis=0, concat_axis=0, tiled=True)  66.6 us
    all_to_all x1, waiting for transfers between devices, per_device(): lax.all_to_all(partial_value, 'expert', split_axis=0, concat_axis=0, tile...  47.9 us
    all_gather x1, waiting for transfers between devices, per_device(): lax.all_gather(dense_grad, 'tensor', axis=0, tiled=True)  42.6 us
    all_gather x1, waiting for transfers between devices, per_device(): lax.all_gather(mixture_grad, 'tensor', axis=0, tiled=True)  40.4 us
    all_gather x1, waiting for transfers between devices, per_device(): normed = lax.all_gather(normed_local, 'tensor', axis=0, tiled=True)  39.8 us
    reduce_scatter x1, waiting for transfers between devices, per_device(): lax.psum_scatter((dense_input + mixture_input).astype(jnp.bfloat16), 'ten...  36.7 us
    reduce_scatter x1, waiting for transfers between devices, per_device(): lax.psum_scatter(mixture_part.astype(jnp.bfloat16), 'tensor', scatter_dim...  36.4 us
  transfers between devices with their start and end apart: 8, of which 7 were waited for; matrix products, arithmetic and copies ran while one was open for 11% of the time, Pallas kernels for 0%

commit v1 on v0

--- a/solution.py
+++ b/solution.py
@@ -22,16 +22,17 @@
     return sigmoid_value * (1.0 + preact * (1.0 - sigmoid_value))
 
 
-def slot_table(group_ids, experts, capacity):
+def route_matrices(group_ids, gates, experts, capacity):
     routes = group_ids.reshape(-1)
-    route_total = routes.shape[0]
-    onehot = (routes[:, None] == jnp.arange(experts, dtype=jnp.int32)[None, :]).astype(jnp.int32)
-    earlier = jnp.cumsum(onehot, axis=0) - onehot
-    slot_index = jnp.sum(earlier * onehot, axis=1)
-    position = routes * capacity + slot_index
-    inverse = jnp.full((experts * capacity,), route_total, jnp.int32)
-    inverse = inverse.at[position].set(jnp.arange(route_total, dtype=jnp.int32))
-    return (position, inverse)
+    order = jnp.arange(routes.shape[0], dtype=jnp.int32)
+    earlier = (routes[:, None] == routes[None, :]) & (order[None, :] < order[:, None])
+    slot_index = jnp.sum(earlier.astype(jnp.int32), axis=1)
+    position = (routes * capacity + slot_index).reshape(group_ids.shape)
+    slots = jnp.arange(experts * capacity, dtype=jnp.int32)
+    held = (position[:, :, None] == slots[None, None, :]).astype(jnp.float32)
+    pick = jnp.sum(held, axis=1).astype(jnp.bfloat16)
+    mix = jnp.sum(held * gates[:, :, None], axis=1)
+    return pick, mix.astype(jnp.bfloat16), jnp.sum(mix, axis=0)
 
 
 def per_device(
@@ -58,9 +59,9 @@
     preact_dense = jnp.einsum("gd,khd->gkh", normed, dense_in, preferred_element_type=jnp.float32)
     hidden_dense = (jax.nn.silu(preact_dense[:, 0]) * preact_dense[:, 1]).astype(jnp.bfloat16)
     dense_part = jnp.dot(hidden_dense, dense_out, preferred_element_type=jnp.float32)
-    position, inverse = slot_table(expert_ids, experts, capacity)
-    padded = jnp.concatenate([normed, jnp.zeros((1, model_width), jnp.bfloat16)], axis=0)
-    buffer = jnp.take(padded, inverse // top_count, axis=0).reshape(experts, capacity, model_width)
+    pick, mix, slot_gates = route_matrices(expert_ids, gate_probs, experts, capacity)
+    buffer = jnp.einsum("gs,gd->sd", pick, normed, preferred_element_type=jnp.float32)
+    buffer = buffer.astype(jnp.bfloat16).reshape(experts, capacity, model_width)
     preact = jnp.einsum(
         "scd,khd->sckh",
         lax.all_to_all(buffer, "expert", split_axis=0, concat_axis=0, tiled=True),
@@ -73,9 +74,8 @@
     )
     partial_value, preact_expert = (partial_value.astype(jnp.bfloat16), preact)
     returned = lax.all_to_all(partial_value, "expert", split_axis=0, concat_axis=0, tiled=True)
-    flat_rows = jnp.take(returned.reshape(experts * capacity, model_width), position, axis=0)
-    flat_rows = flat_rows.reshape(group_rows, top_count, model_width)
-    mixture_part = jnp.sum(flat_rows.astype(jnp.float32) * gate_probs[:, :, None], axis=1)
+    returned = returned.reshape(experts * capacity, model_width)
+    mixture_part = jnp.dot(mix, returned, preferred_element_type=jnp.float32)
     dense_raw, mixture_raw = (
         lax.psum_scatter(
             dense_part.astype(jnp.bfloat16), "tensor", scatter_dimension=0, tiled=True
@@ -104,12 +104,9 @@
     dense_input = jnp.dot(gate_dense, dense_in[0], preferred_element_type=jnp.float32) + jnp.dot(
         up_dense, dense_in[1], preferred_element_type=jnp.float32
     )
-    scaled = (gate_probs[:, :, None] * mixture_rows[:, None, :].astype(jnp.float32)).astype(
-        jnp.bfloat16
-    )
-    scaled = scaled.reshape(group_rows * top_count, model_width)
-    padded_grad = jnp.concatenate([scaled, jnp.zeros((1, model_width), jnp.bfloat16)], axis=0)
-    grad_buffer = jnp.take(padded_grad, inverse, axis=0).reshape(experts, capacity, model_width)
+    grad_buffer = jnp.einsum("gs,gd->sd", pick, mixture_rows, preferred_element_type=jnp.float32)
+    grad_buffer = (grad_buffer * slot_gates[:, None]).astype(jnp.bfloat16)
+    grad_buffer = grad_buffer.reshape(experts, capacity, model_width)
     back_expert = jnp.einsum(
         "scd,hd->sch",
         lax.all_to_all(grad_buffer, "expert", split_axis=0, concat_axis=0, tiled=True),
@@ -125,10 +122,8 @@
         + jnp.einsum("sch,hd->scd", up_expert, weight_in[1], preferred_element_type=jnp.float32)
     ).astype(jnp.bfloat16)
     returned_grad = lax.all_to_all(input_part, "expert", split_axis=0, concat_axis=0, tiled=True)
-    grad_rows = jnp.take(returned_grad.reshape(experts * capacity, model_width), position, axis=0)
-    mixture_input = jnp.sum(
-        grad_rows.reshape(group_rows, top_count, model_width).astype(jnp.float32), axis=1
-    )
+    returned_grad = returned_grad.reshape(experts * capacity, model_width)
+    mixture_input = jnp.dot(pick, returned_grad, preferred_element_type=jnp.float32)
     input_total = lax.psum_scatter(
         (dense_input + mixture_input).astype(jnp.bfloat16),
         "tensor",

time: 654 us -> 522 us (0.80); the launches traced: 645 us -> 521 us
  local copies, waits for them, and re-layouts: 90.4 us -> 3.63 us
  other arithmetic: 58.7 us -> 12.9 us
  matrix products: 85.9 us -> 96.9 us
    gather x4 -> x0, local copies, waits for them, and re-layouts: 45 us -> none  [the longest x1 15.8 us: per_device(): jnp.take(padded_grad, inverse, axis=0)]
    reduce_sum x3 -> x2, other arithmetic: 24.8 us -> 1.02 us  [the longest x1 0.84 us: route_matrices(): return (pick, mix.astype(jnp.bfloat16), jnp.sum(mix, axis=0))]
    convert_element_type x2 -> x0, local copies, waits for them, and re-layouts: 18.7 us -> none  [the longest x1 9.46 us: per_device(): grad_rows.reshape(group_rows, top_count, model_width).astype(jnp.float32)]
    dot_general x0 -> x4, matrix products: none -> 17.4 us  [the longest x1 6.03 us: per_device(): jnp.dot(pick, returned_grad, preferred_element_type=jnp.float32)]
    mul x5 -> x0, local copies, waits for them, and re-layouts: 16.7 us -> none  [the longest x2 16.3 us: per_device(): gate_probs[:, :, None] * mixture_rows[:, None, :].astype(jnp.float32)]
    convert_element_type x5 -> x1, other arithmetic: 17.8 us -> 2.86 us  [per_device(): norm_grad(mixture_raw, norm_gains[2], upstream).astype(jnp.bfloat16)]
  transfers between devices with their start and end apart: 8 -> 8, of which waited for: 7 -> 7; matrix products, arithmetic and copies ran while one was open for 11% -> 7% of each run, Pallas kernels for 0% -> 0%
where the time goes in v1:
time: 522 us; the launch traced here: 521 us
  waiting for transfers between devices  250 us (48%)
  blocking collectives  133 us (25%)
  matrix products  96.9 us (19%)
  between operations  14.4 us (3%)
  other arithmetic  12.9 us (2%)
  starting transfers between devices  10.1 us (2%)
    all_to_all x1, blocking collectives, per_device(): lax.all_to_all(grad_buffer, 'expert', split_axis=0, concat_axis=0, tiled=...  66.7 us
    all_to_all x1, blocking collectives, per_device(): lax.all_to_all(buffer, 'expert', split_axis=0, concat_axis=0, tiled=True)  66.6 us
    all_to_all x1, waiting for transfers between devices, per_device(): lax.all_to_all(partial_value, 'expert', split_axis=0, concat_axis=0, tile...  48 us
    all_gather x1, waiting for transfers between devices, per_device(): lax.all_gather(dense_grad, 'tensor', axis=0, tiled=True)  42 us
    all_gather x1, waiting for transfers between devices, per_device(): normed = lax.all_gather(normed_local, 'tensor', axis=0, tiled=True)  41.4 us
    all_gather x1, waiting for transfers between devices, per_device(): lax.all_gather(mixture_grad, 'tensor', axis=0, tiled=True)  40.7 us
    reduce_scatter x1, waiting for transfers between devices, per_device(): lax.psum_scatter((dense_input + mixture_input).astype(jnp.bfloat16), 'ten...  36.7 us
    reduce_scatter x1, waiting for transfers between devices, per_device(): lax.psum_scatter(mixture_part.astype(jnp.bfloat16), 'tensor', scatter_dim...  36.6 us
  transfers between devices with their start and end apart: 8, of which 7 were waited for; matrix products, arithmetic and copies ran while one was open for 7% of the time, Pallas kernels for 0%

profile of v1, /device:TPU:0, one launch (start us, length us, event | category | flops | bytes accessed | tf_op | source)
XLA Modules:
  0.0 521.5 jit_solution(6669368352036570022)
XLA Ops:
  8.3 1.2 fusion.64
  9.6 2.0 fusion.45
  14.4 41.4 %all-gather.4.cloned.1.call-done = bf16[128,7168]{1,0:T(8,128)(2,1)} async-done(((bf16[32,7168]{1,0:T(8,128)(2,1)}), bf16[128,7168]{1,0:T(8,128)(2,1)}) %all-gather.4.cloned.1.call-update) | async-done | bytes 1835024 | tf_op jit(solution)/shard_map/all_gather | solution.py:58
  55.8 3.1 convolution_convert_fusion.1
  58.9 66.6 %all_to_all.20 = bf16[8,48,7168]{2,1,0:T(8,128)(2,1)S(1)} all-to-all(bf16[8,48,7168]{2,1,0:T(8,128)(2,1)S(1)} %bitcast.142), channel_id=1, replica_groups=mesh['expert'=8,'tensor'=4] {'expert'}, dimensions={0} | all-to-all | bytes 11010048 | tf_op jit(solution)/shard_map/all_to_all | solution.py:67
  125.5 12.4 %fusion = f32[8,48,2,608]{3,1,2,0:T(8,128)S(1)} fusion(bf16[1,2,608,7168]{3,2,1,0:T(8,128)(2,1)} %param.12, bf16[8,48,7168]{2,1,0:T(8,128)(2,1)S(1)} %all_to_all.20), kind=kOutput, calls=%fused_computation | convolution fusion | flops 6694109184 | bytes 24805376 | tf_op jit(solution)/shard_map/scd,khd->sckh/dot_general | solution.py:65
  137.9 1.3 copy-done.3
  139.2 9.8 %convolution_convert_fusion = bf16[8,48,7168]{2,1,0:T(8,128)(2,1)} fusion(bf16[1,608,7168]{2,1,0:T(8,128)(2,1)} %param.13, f32[8,48,2,608]{3,1,2,0:T(8,128)S(1)} %fusion), kind=kOutput, calls=%fused_computation.4 | convolution fusion | flops 3351207936 | bytes 16089088 | tf_op jit(solution)/shard_map/sch,hd->scd/dot_general | solution.py:72
  149.0 4.8 all-to-all-start.1
  153.9 8.4 %fusion.21 = f32[128,2,608]{0,2,1:T(8,128)S(1)} fusion(bf16[2,608,7168]{2,1,0:T(8,128)(2,1)} %param.10, bf16[128,7168]{1,0:T(8,128)(2,1)S(1)} %copy-done.1), kind=kOutput, calls=%fused_computation.26 | convolution fusion | flops 2231369728 | bytes 19890176 | tf_op jit(solution)/shard_map/gd,khd->gkh/dot_general | solution.py:59
  162.3 6.4 %convolution_convert_fusion.3 = bf16[128,7168]{1,0:T(8,128)(2,1)} fusion(bf16[608,7168]{1,0:T(8,128)(2,1)} %param.11, f32[128,2,608]{0,2,1:T(8,128)S(1)} %fusion.21), kind=kOutput, calls=%fused_computation.24 | convolution fusion | flops 1117069312 | bytes 11173888 | tf_op jit(solution)/shard_map/dot_general | solution.py:61
  169.0 48.0 %all-to-all-done.1 = bf16[8,48,7168]{2,1,0:T(8,128)(2,1)} async-done(((bf16[8,48,7168]{2,1,0:T(8,128)(2,1)}), bf16[8,48,7168]{2,1,0:T(8,128)(2,1)}, u32[]{:S(2)}, u32[]{:S(2)}) %all-to-all-start.1) | async-done | bytes 5505056 | tf_op jit(solution)/shard_map/all_to_all | solution.py:76
  217.0 5.0 convolution_convert_fusion.2
  222.1 36.6 %reduce-scatter.6.cloned.1.call-done = bf16[32,7168]{1,0:T(8,128)(2,1)} async-done(((bf16[128,7168]{1,0:T(8,128)(2,1)}), bf16[32,7168]{1,0:T(8,128)(2,1)}) %reduce-scatter.6.cloned.1.call-update) | async-done | bytes 458768 | tf_op jit(solution)/shard_map/reduce_scatter | solution.py:83
  258.7 1.7 fusion.63
  260.5 2.9 fusion.55
  263.3 40.7 %all-gather.8.cloned.1.call-done = bf16[128,7168]{1,0:T(8,128)(2,1)} async-done(((bf16[32,7168]{1,0:T(8,128)(2,1)}), bf16[128,7168]{1,0:T(8,128)(2,1)}) %all-gather.8.cloned.1.call-update) | async-done | bytes 1835024 | tf_op jit(solution)/shard_map/all_gather | solution.py:97
  304.0 3.3 multiply_convert_fusion
  307.3 66.7 %all_to_all.21 = bf16[8,48,7168]{2,1,0:T(8,128)(2,1)S(1)} all-to-all(bf16[8,48,7168]{2,1,0:T(8,128)(2,1)S(1)} %bitcast.141), channel_id=1, replica_groups=mesh['expert'=8,'tensor'=4] {'expert'}, dimensions={0} | all-to-all | bytes 11010048 | tf_op jit(solution)/shard_map/all_to_all | solution.py:112
  374.0 4.5 fusion.9
  378.5 10.8 %fusion.3 = f32[8,48,7168]{2,1,0:T(8,128)} fusion(bf16[1,2,608,7168]{3,2,1,0:T(8,128)(2,1)} %param.12, f32[8,48,608]{2,1,0:T(8,128)S(1)} %fusion.9, f32[8,48,2,608]{3,1,2,0:T(8,128)S(1)} %copy-done.4), kind=kOutput, calls=%fused_computation.7 | convolution fusion | flops 3349389312 | bytes 22528000 | tf_op jit(solution)/shard_map/sch,hd->scd/dot_general | solution.py:121
  389.3 11.4 %add_convert_fusion = bf16[8,48,7168]{2,1,0:T(8,128)(2,1)} fusion(f32[8,48,7168]{2,1,0:T(8,128)} %fusion.3, bf16[1,2,608,7168]{3,2,1,0:T(8,128)(2,1)} %param.12, f32[8,48,608]{2,1,0:T(8,128)S(1)} %fusion.9, f32[8,48,2,608]{3,1,2,0:T(8,128)S(1)} %copy-done.4), kind=kOutput, calls=%fused_computation.2 | convolution fusion | flops 3353960448 | bytes 27197440 | tf_op jit(solution)/shard_map/sch,hd->scd/dot_general | solution.py:122
  400.7 4.7 all-to-all-start.3
  406.2 42.0 %all-gather.6.cloned.1.call-done = bf16[128,7168]{1,0:T(8,128)(2,1)} async-done(((bf16[32,7168]{1,0:T(8,128)(2,1)}), bf16[128,7168]{1,0:T(8,128)(2,1)}) %all-gather.6.cloned.1.call-update) | async-done | bytes 1835024 | tf_op jit(solution)/shard_map/all_gather | solution.py:96
  448.2 6.6 %fusion.88 = f32[128,608]{0,1:T(8,128)S(1)} fusion(bf16[128,7168]{1,0:T(8,128)(2,1)} %all-gather.6.cloned.1.call-done, bf16[608,7168]{1,0:T(8,128)(2,1)} %param.11), kind=kOutput, calls=%fused_computation.126 | convolution fusion | flops 1115684864 | bytes 10862592 | tf_op jit(solution)/shard_map/gd,hd->gh/dot_general | solution.py:99
  454.8 5.4 %fusion.5 = f32[128,7168]{1,0:T(8,128)S(1)} fusion(bf16[2,608,7168]{2,1,0:T(8,128)(2,1)} %param.10, f32[128,608]{0,1:T(8,128)S(1)} %fusion.88, f32[128,2,608]{0,2,1:T(8,128)S(1)} %fusion.21), kind=kOutput, calls=%fused_computation.9 | convolution fusion | flops 1116151808 | bytes 13008896 | tf_op jit(solution)/shard_map/dot_general | solution.py:104
  460.3 3.8 fusion.16
  464.1 4.4 all-to-all-done.3
  468.5 6.0 %fusion.19 = bf16[128,7168]{1,0:T(8,128)(2,1)} fusion(f32[128,7168]{1,0:T(8,128)} %fusion.16, bf16[384,7168]{1,0:T(8,128)(2,1)} %bitcast.25, bf16[128,384]{1,0:T(8,128)(2,1)S(1)} %get-tuple-element.8), kind=kOutput, calls=%fused_computation.22 | convolution fusion | flops 706478080 | bytes 11108352 | tf_op jit(solution)/shard_map/dot_general | solution.py:126
  474.6 36.7 %reduce-scatter.8.cloned.1.call-done = bf16[32,7168]{1,0:T(8,128)(2,1)} async-done(((bf16[128,7168]{1,0:T(8,128)(2,1)}), bf16[32,7168]{1,0:T(8,128)(2,1)}) %reduce-scatter.8.cloned.1.call-update) | async-done | bytes 458768 | tf_op jit(solution)/shard_map/reduce_scatter | solution.py:127
  511.2 1.3 fusion.65
  512.5 2.1 fusion.49
  (52 shorter events, 5.4 us)
Async XLA Ops:
  7.2 48.7 %all-gather.4.cloned.1.call-start = ((), (), s32[]{:S(2)}) async-start(), calls=%async_computation.7 | async-start | bytes 2293760 | tf_op jit(solution)/shard_map/all_gather | solution.py:58
  137.9 1.3 copy-start.3
  149.0 4.9 copy-start.1
  149.0 68.0 %all-to-all-start.1 = ((bf16[8,48,7168]{2,1,0:T(8,128)(2,1)}), bf16[8,48,7168]{2,1,0:T(8,128)(2,1)}, u32[]{:S(2)}, u32[]{:S(2)}) async-start(bf16[8,48,7168]{2,1,0:T(8,128)(2,1)} %convolution_convert_fusion), calls=%async_computation.2 | async-start | bytes 11010048 | tf_op jit(solution)/shard_map/all_to_all | solution.py:76
  153.9 68.3 %reduce-scatter.4.cloned.1.call-start = ((), (), s32[]{:S(2)}) async-start(), calls=%async_computation.8 | async-start | bytes 2293760 | tf_op jit(solution)/shard_map/reduce_scatter | solution.py:80
  168.7 90.0 %reduce-scatter.6.cloned.1.call-start = ((), (), s32[]{:S(2)}) async-start(), calls=%async_computation.9 | async-start | bytes 2293760 | tf_op jit(solution)/shard_map/reduce_scatter | solution.py:83
  217.0 41.7 %copy-start.2 = (bf16[32,7168]{1,0:T(8,128)(2,1)S(1)}, bf16[32,7168]{1,0:T(8,128)(2,1)}, u32[]{:S(2)}) copy-start(bf16[32,7168]{1,0:T(8,128)(2,1)} %param.17) | copy-start | bytes 1376260
  217.0 43.4 %copy-start = (bf16[32,7168]{1,0:T(8,128)(2,1)S(1)}, bf16[32,7168]{1,0:T(8,128)(2,1)}, u32[]{:S(2)}) copy-start(bf16[32,7168]{1,0:T(8,128)(2,1)} %param.9) | copy-start | bytes 1376260
  222.1 82.0 %all-gather.8.cloned.1.call-start = ((), (), s32[]{:S(2)}) async-start(), calls=%async_computation.11 | async-start | bytes 2293760 | tf_op jit(solution)/shard_map/all_gather | solution.py:97
  304.0 70.0 %slice-start.5 = ((s8[8716288]{0:T(1024)(128)(4,1)}), s8[4194304]{0:T(1024)(128)(4,1)S(1)}, s32[]{:S(2)}) async-start(s8[8716288]{0:T(1024)(128)(4,1)} %bitcast.150), calls=%async_computation.18 | async-start | bytes 8388608
  304.0 70.0 %slice-start.6 = ((s8[8716288]{0:T(1024)(128)(4,1)}), s8[4194304]{0:T(1024)(128)(4,1)S(1)}, s32[]{:S(2)}) async-start(s8[8716288]{0:T(1024)(128)(4,1)} %bitcast.150), calls=%async_computation.19 | async-start | bytes 8388608
  307.3 66.7 %slice-start.7 = ((s8[8716288]{0:T(1024)(128)(4,1)}), s8[327680]{0:T(1024)(128)(4,1)S(1)}, s32[]{:S(2)}) async-start(s8[8716288]{0:T(1024)(128)(4,1)} %bitcast.150), calls=%async_computation.20 | async-start | bytes 655360
  374.0 4.5 copy-start.4
  400.7 67.8 %all-to-all-start.3 = ((bf16[8,48,7168]{2,1,0:T(8,128)(2,1)}), bf16[8,48,7168]{2,1,0:T(8,128)(2,1)}, u32[]{:S(2)}, u32[]{:S(2)}) async-start(bf16[8,48,7168]{2,1,0:T(8,128)(2,1)} %add_convert_fusion), calls=%async_computation.5 | async-start | bytes 11010048 | tf_op jit(solution)/shard_map/all_to_all | solution.py:124
  405.4 42.8 %all-gather.6.cloned.1.call-start = ((), (), s32[]{:S(2)}) async-start(), calls=%async_computation.10 | async-start | bytes 2293760 | tf_op jit(solution)/shard_map/all_gather | solution.py:96
  405.9 105.3 %reduce-scatter.8.cloned.1.call-start = ((), (), s32[]{:S(2)}) async-start(), calls=%async_computation.12 | async-start | bytes 2293760 | tf_op jit(solution)/shard_map/reduce_scatter | solution.py:127
  448.2 12.0 %slice-start = ((s8[17432576]{0:T(1024)(128)(4,1)}), s8[4194304]{0:T(1024)(128)(4,1)S(1)}, s32[]{:S(2)}) async-start(s8[17432576]{0:T(1024)(128)(4,1)} %bitcast.139), calls=%async_computation.13 | async-start | bytes 8388608
  448.2 12.0 %slice-start.1 = ((s8[17432576]{0:T(1024)(128)(4,1)}), s8[4194304]{0:T(1024)(128)(4,1)S(1)}, s32[]{:S(2)}) async-start(s8[17432576]{0:T(1024)(128)(4,1)} %bitcast.139), calls=%async_computation.14 | async-start | bytes 8388608
  448.2 12.0 %slice-start.2 = ((s8[17432576]{0:T(1024)(128)(4,1)}), s8[4194304]{0:T(1024)(128)(4,1)S(1)}, s32[]{:S(2)}) async-start(s8[17432576]{0:T(1024)(128)(4,1)} %bitcast.139), calls=%async_computation.15 | async-start | bytes 8388608
  454.8 5.5 %slice-start.3 = ((s8[17432576]{0:T(1024)(128)(4,1)}), s8[4194304]{0:T(1024)(128)(4,1)S(1)}, s32[]{:S(2)}) async-start(s8[17432576]{0:T(1024)(128)(4,1)} %bitcast.139), calls=%async_computation.16 | async-start | bytes 8388608
  454.8 5.5 %slice-start.4 = ((s8[17432576]{0:T(1024)(128)(4,1)}), s8[655360]{0:T(1024)(128)(4,1)S(1)}, s32[]{:S(2)}) async-start(s8[17432576]{0:T(1024)(128)(4,1)} %bitcast.139), calls=%async_computation.17 | async-start | bytes 1310720
Sparse Core Ops, SparseCore 0:
  11.7 44.0 all-gather.3
  168.9 38.6 reduce-scatter.3
  222.2 36.4 reduce-scatter.5
  263.5 40.5 all-gather.7
  407.5 40.6 all-gather.5
  474.7 36.4 reduce-scatter.7

commit v2 on v1

--- a/solution.py
+++ b/solution.py
@@ -1,6 +1,10 @@
+import functools
+
 import jax
 import jax.numpy as jnp
 from jax import lax
+from jax.experimental import pallas as pl
+from jax.experimental.pallas import tpu as pltpu
 from jax.sharding import PartitionSpec as P
 
 epsilon = 1e-05
@@ -33,6 +37,156 @@
     pick = jnp.sum(held, axis=1).astype(jnp.bfloat16)
     mix = jnp.sum(held * gates[:, :, None], axis=1)
     return pick, mix.astype(jnp.bfloat16), jnp.sum(mix, axis=0)
+
+
+def spread_kernel(experts, ranks, chunks, separate, *refs):
+    if separate:
+        rows, pick, gates, extra, received, whole, *scratch = refs
+    else:
+        rows, pick, gates, received, whole, *scratch = refs
+        extra = None
+    staged, outgoing, z_send, z_recv, e_send, e_recv, w_send, w_recv, own_sem, stage_sem = scratch
+    me, rank = lax.axis_index("expert"), lax.axis_index("tensor")
+    mesh_id = pl.DeviceIdType.MESH
+    width = rows.shape[1] // chunks
+    group_rows = ranks * rows.shape[0]
+
+    barrier = pltpu.get_barrier_semaphore()
+    for k in range(1, ranks):
+        pl.semaphore_signal(
+            barrier, inc=1, device_id={"tensor": lax.rem(rank + k, ranks)}, device_id_type=mesh_id
+        )
+    for k in range(1, experts):
+        pl.semaphore_signal(
+            barrier, inc=1, device_id={"expert": lax.rem(me + k, experts)}, device_id_type=mesh_id
+        )
+    pl.semaphore_wait(barrier, ranks + experts - 2)
+
+    def gather_copy(c, k, slot):
+        cols = pl.ds(c * width, width)
+        return pltpu.make_async_remote_copy(
+            src_ref=rows.at[:, cols],
+            dst_ref=staged.at[slot, :, cols],
+            send_sem=z_send.at[c, k],
+            recv_sem=z_recv.at[c, k],
+            device_id={"tensor": lax.rem(rank + k, ranks)},
+            device_id_type=mesh_id,
+        )
+
+    def expert_copy(c, k, slot):
+        cols = pl.ds(c * width, width)
+        target = lax.rem(me + k, experts)
+        return pltpu.make_async_remote_copy(
+            src_ref=outgoing.at[target, :, cols],
+            dst_ref=received.at[slot, :, cols],
+            send_sem=e_send.at[c, k],
+            recv_sem=e_recv.at[c, k],
+            device_id={"expert": target},
+            device_id_type=mesh_id,
+        )
+
+    def extra_copy(k, slot):
+        return pltpu.make_async_remote_copy(
+            src_ref=extra,
+            dst_ref=whole.at[slot],
+            send_sem=w_send.at[k],
+            recv_sem=w_recv.at[k],
+            device_id={"tensor": lax.rem(rank + k, ranks)},
+            device_id_type=mesh_id,
+        )
+
+    for c in range(chunks):
+        for k in range(1, ranks):
+            gather_copy(c, k, rank).start()
+    staged[rank] = rows[...]
+    for c in range(chunks):
+        cols = slice(c * width, (c + 1) * width)
+        for k in range(1, ranks):
+            gather_copy(c, k, lax.rem(rank + ranks - k, ranks)).wait_recv()
+        if c == chunks - 1:
+            if separate:
+                for k in range(1, ranks):
+                    extra_copy(k, rank).start()
+                stage_copy = pltpu.make_async_copy(extra, whole.at[rank], stage_sem)
+            else:
+                stage_copy = pltpu.make_async_copy(staged, whole, stage_sem)
+            stage_copy.start()
+        block = staged[:, :, cols].reshape(group_rows, width)
+
+        def fill(target):
+            value = jnp.dot(pick[target], block, preferred_element_type=jnp.float32)
+            if separate:
+                value = value * gates[target]
+            outgoing[target, :, cols] = value.astype(outgoing.dtype)
+
+        def step(k, carry):
+            fill(lax.rem(me + k, experts))
+            expert_copy(c, k, me).start()
+            return carry
+
+        lax.fori_loop(1, experts, step, 0)
+        fill(me)
+    own_copy = pltpu.make_async_copy(outgoing.at[me], received.at[me], own_sem)
+    own_copy.start()
+    for c in range(chunks):
+        for k in range(1, ranks):
+            gather_copy(c, k, rank).wait_send()
+
+        def finish(k, carry):
+            copy = expert_copy(c, k, lax.rem(me + experts - k, experts))
+            copy.wait_send()
+            copy.wait_recv()
+            return carry
+
+        lax.fori_loop(1, experts, finish, 0)
+    if separate:
+        for k in range(1, ranks):
+            copy = extra_copy(k, lax.rem(rank + ranks - k, ranks))
+            copy.wait_send()
+            copy.wait_recv()
+    stage_copy.wait()
+    own_copy.wait()
+
+
+def spread(rows, pick, gates, extra, experts, collective_id):
+    ranks = lax.axis_size("tensor")
+    count, model_width = rows.shape
+    capacity = pick.shape[1] // experts
+    chunks = 4 if model_width % 512 == 0 else 1
+    separate = extra is not None
+    dma = pltpu.SemaphoreType.DMA
+    operands = [
+        rows,
+        pick.T.reshape(experts, capacity, pick.shape[0]),
+        gates.reshape(experts, capacity, 1),
+    ]
+    if separate:
+        operands.append(extra)
+    received, whole = pl.pallas_call(
+        functools.partial(spread_kernel, experts, ranks, chunks, separate),
+        out_shape=(
+            jax.ShapeDtypeStruct((experts, capacity, model_width), rows.dtype),
+            jax.ShapeDtypeStruct((ranks, count, model_width), rows.dtype),
+        ),
+        in_specs=[pl.BlockSpec(memory_space=pltpu.VMEM)] * len(operands),
+        out_specs=(pl.BlockSpec(memory_space=pl.ANY), pl.BlockSpec(memory_space=pl.ANY)),
+        scratch_shapes=[
+            pltpu.VMEM((ranks, count, model_width), rows.dtype),
+            pltpu.VMEM((experts, capacity, model_width), rows.dtype),
+            dma((chunks, ranks)),
+            dma((chunks, ranks)),
+            dma((chunks, experts)),
+            dma((chunks, experts)),
+            dma((ranks,)),
+            dma((ranks,)),
+            dma(()),
+            dma(()),
+        ],
+        compiler_params=pltpu.CompilerParams(
+            collective_id=collective_id, has_side_effects=True, vmem_limit_bytes=40 * 1024 * 1024
+        ),
+    )(*operands)
+    return received, whole.reshape(ranks * count, model_width)
 
 
 def per_device(
@@ -55,16 +209,14 @@
     weight_out = expert_out[0]
     source = tokens.astype(jnp.float32)
     normed_local = (source * rms_scale(source) * norm_gains[0]).astype(jnp.bfloat16)
-    normed = lax.all_gather(normed_local, "tensor", axis=0, tiled=True)
+    pick, mix, slot_gates = route_matrices(expert_ids, gate_probs, experts, capacity)
+    arrived, normed = spread(normed_local, pick, slot_gates, None, experts, 0)
     preact_dense = jnp.einsum("gd,khd->gkh", normed, dense_in, preferred_element_type=jnp.float32)
     hidden_dense = (jax.nn.silu(preact_dense[:, 0]) * preact_dense[:, 1]).astype(jnp.bfloat16)
     dense_part = jnp.dot(hidden_dense, dense_out, preferred_element_type=jnp.float32)
-    pick, mix, slot_gates = route_matrices(expert_ids, gate_probs, experts, capacity)
-    buffer = jnp.einsum("gs,gd->sd", pick, normed, preferred_element_type=jnp.float32)
-    buffer = buffer.astype(jnp.bfloat16).reshape(experts, capacity, model_width)
     preact = jnp.einsum(
         "scd,khd->sckh",
-        lax.all_to_all(buffer, "expert", split_axis=0, concat_axis=0, tiled=True),
+        arrived,
         weight_in,
         preferred_element_type=jnp.float32,
     )
@@ -92,10 +244,7 @@
     upstream = cotangent.astype(jnp.float32)
     dense_grad = norm_grad(dense_raw, norm_gains[1], upstream).astype(jnp.bfloat16)
     mixture_grad = norm_grad(mixture_raw, norm_gains[2], upstream).astype(jnp.bfloat16)
-    dense_rows, mixture_rows = (
-        lax.all_gather(dense_grad, "tensor", axis=0, tiled=True),
-        lax.all_gather(mixture_grad, "tensor", axis=0, tiled=True),
-    )
+    arrived_grad, dense_rows = spread(mixture_grad, pick, slot_gates, dense_grad, experts, 1)
     back_dense = jnp.einsum("gd,hd->gh", dense_rows, dense_out, preferred_element_type=jnp.float32)
     gate_dense = (back_dense * preact_dense[:, 1] * silu_grad(preact_dense[:, 0])).astype(
         jnp.bfloat16
@@ -104,12 +253,9 @@
     dense_input = jnp.dot(gate_dense, dense_in[0], preferred_element_type=jnp.float32) + jnp.dot(
         up_dense, dense_in[1], preferred_element_type=jnp.float32
     )
-    grad_buffer = jnp.einsum("gs,gd->sd", pick, mixture_rows, preferred_element_type=jnp.float32)
-    grad_buffer = (grad_buffer * slot_gates[:, None]).astype(jnp.bfloat16)
-    grad_buffer = grad_buffer.reshape(experts, capacity, model_width)
     back_expert = jnp.einsum(
         "scd,hd->sch",
-        lax.all_to_all(grad_buffer, "expert", split_axis=0, concat_axis=0, tiled=True),
+        arrived_grad,
         weight_out,
         preferred_element_type=jnp.float32,
     )

time: 522 us -> 471 us (0.902)
  Pallas kernels: 0 us -> 150 us
  blocking collectives: 133 us -> 0 us
  waiting for transfers between devices: 250 us -> 188 us
    pallas_call x0 -> x2, Pallas kernels: none -> 150 us  [spread(): pl.pallas_call(functools.partial(spread_kernel, experts, ranks, chunks, s...]
    all_to_all x2 -> x0, blocking collectives: 133 us -> none  [the longest x1 66.7 us: per_device(): lax.all_to_all(grad_buffer, 'expert', split_axis=0, concat_axis=0, tiled=...]
    all_gather x3 -> x0, waiting for transfers between devices: 124 us -> none  [the longest x1 42 us: per_device(): lax.all_gather(dense_grad, 'tensor', axis=0, tiled=True)]
    all_to_all x1, waiting for transfers between devices: 4.45 us -> 47.5 us  [per_device(): lax.all_to_all(input_part, 'expert', split_axis=0, concat_axis=0, tiled=T...]
    reduce_scatter x1, waiting for transfers between devices: 36.7 us -> 48.8 us  [per_device(): lax.psum_scatter((dense_input + mixture_input).astype(jnp.bfloat16), 'ten...]
    reduce_scatter x1, waiting for transfers between devices: 36.6 us -> 43.3 us  [per_device(): lax.psum_scatter(mixture_part.astype(jnp.bfloat16), 'tensor', scatter_dim...]
    dot_general x4 -> x2, matrix products: 23.3 us -> 19.5 us  [the longest x1 12.4 us: per_device(): jnp.einsum('scd,khd->sckh', arrived, weight_in, preferred_element_type=jn...]
  transfers between devices with their start and end apart: 8 -> 5, of which waited for: 7 -> 4; matrix products, arithmetic and copies ran while one was open for 7% -> 7% of each run, Pallas kernels for 0% -> 0%
where the time goes in v2:
time: 471 us; the launch traced here: 470 us
  waiting for transfers between devices  188 us (40%)
  Pallas kernels  150 us (32%)
  matrix products  92.6 us (20%)
  between operations  14 us (3%)
  other arithmetic  11.9 us (3%)
  starting transfers between devices  9.87 us (2%)
    pallas_call x2, Pallas kernels, spread(): pl.pallas_call(functools.partial(spread_kernel, experts, ranks, chunks, s...  150 us
    reduce_scatter x1, waiting for transfers between devices, per_device(): lax.psum_scatter((dense_input + mixture_input).astype(jnp.bfloat16), 'ten...  48.8 us
    all_to_all x1, waiting for transfers between devices, per_device(): lax.all_to_all(partial_value, 'expert', split_axis=0, concat_axis=0, tile...  48.2 us
    all_to_all x1, waiting for transfers between devices, per_device(): lax.all_to_all(input_part, 'expert', split_axis=0, concat_axis=0, tiled=T...  47.5 us
    reduce_scatter x1, waiting for transfers between devices, per_device(): lax.psum_scatter(mixture_part.astype(jnp.bfloat16), 'tensor', scatter_dim...  43.3 us
    dot_general x1, matrix products, per_device(): jnp.einsum('scd,khd->sckh', arrived, weight_in, preferred_element_type=jn...  12.4 us
    dot_general x1, matrix products, per_device(): jnp.einsum('sch,hd->scd', up_expert, weight_in[1], preferred_element_type...  11.4 us
    dot_general x1, matrix products, per_device(): jnp.einsum('sch,hd->scd', gate_expert, weight_in[0], preferred_element_ty...  10.8 us
  transfers between devices with their start and end apart: 5, of which 4 were waited for; matrix products, arithmetic and copies ran while one was open for 7% of the time, Pallas kernels for 0%

profile of v2, /device:TPU:0, one launch (start us, length us, event | category | flops | bytes accessed | tf_op | source)
XLA Modules:
  0.0 470.4 jit_solution(7742988419313967708)
XLA Ops:
  7.2 1.1 fusion.83
  8.3 1.2 fusion.62
  9.5 0.8 copy.32
  10.9 0.7 multiply_add_fusion
  11.6 0.8 select_reduce_fusion
  12.8 1.2 fusion.43.refs_0_
  14.0 75.3 %shard_map.104 = (bf16[8,48,7168]{2,1,0:T(8,128)(2,1)S(1)}, bf16[4,32,7168]{2,1,0:T(8,128)(2,1)S(1)}) custom-call(bf16[32,7168]{1,0:T(8,128)(2,1)S(1)} %fusion.43.refs_0_, bf16[8,48,128]{2,1,0:T(8,128)(2,1)S(1)} %bitcast.141, f32[8,48,1]{2,1,0:T(8,128)S(1)} %reshape.87.refs_2_), custom_call_target="tpu_custom_call" | custom-call | tf_op jit(solution)/shard_map/pallas_call | solution.py:165
  89.3 12.4 %fusion = f32[8,48,2,608]{3,1,2,0:T(8,128)S(1)} fusion(bf16[1,2,608,7168]{3,2,1,0:T(8,128)(2,1)} %param.12, bf16[8,48,7168]{2,1,0:T(8,128)(2,1)S(1)} %get-tuple-element.7), kind=kOutput, calls=%fused_computation | convolution fusion | flops 6694109184 | bytes 24805376 | tf_op jit(solution)/shard_map/scd,khd->sckh/dot_general | solution.py:217
  101.7 1.3 copy-done.2
  103.0 9.8 %convolution_convert_fusion = bf16[8,48,7168]{2,1,0:T(8,128)(2,1)} fusion(bf16[1,608,7168]{2,1,0:T(8,128)(2,1)} %param.13, f32[8,48,2,608]{3,1,2,0:T(8,128)S(1)} %fusion), kind=kOutput, calls=%fused_computation.3 | convolution fusion | flops 3351207936 | bytes 16089088 | tf_op jit(solution)/shard_map/sch,hd->scd/dot_general | solution.py:224
  112.8 4.7 all-to-all-start
  117.5 8.4 %fusion.84 = f32[128,2,608]{0,2,1:T(8,128)S(1)} fusion(bf16[128,7168,1]{1,0,2:T(8,128)(2,1)S(1)} %bitcast.140, bf16[2,608,7168]{2,1,0:T(8,128)(2,1)} %param.10), kind=kOutput, calls=%fused_computation.121 | convolution fusion | flops 2231369728 | bytes 19890176 | tf_op jit(solution)/shard_map/gd,khd->gkh/dot_general | solution.py:214
  126.0 6.4 %convolution_convert_fusion.2 = bf16[128,7168]{1,0:T(8,128)(2,1)} fusion(bf16[608,7168]{1,0:T(8,128)(2,1)} %param.11, f32[128,2,608]{0,2,1:T(8,128)S(1)} %fusion.84), kind=kOutput, calls=%fused_computation.22 | convolution fusion | flops 1117069312 | bytes 11173888 | tf_op jit(solution)/shard_map/dot_general | solution.py:216
  132.6 48.2 %all-to-all-done = bf16[8,48,7168]{2,1,0:T(8,128)(2,1)} async-done(((bf16[8,48,7168]{2,1,0:T(8,128)(2,1)}), bf16[8,48,7168]{2,1,0:T(8,128)(2,1)}, u32[]{:S(2)}, u32[]{:S(2)}) %all-to-all-start) | async-done | bytes 5505056 | tf_op jit(solution)/shard_map/all_to_all | solution.py:228
  180.8 5.1 %convolution_convert_fusion.1 = bf16[128,7168]{1,0:T(8,128)(2,1)} fusion(bf16[384,7168]{1,0:T(8,128)(2,1)} %bitcast.16, bf16[128,384]{1,0:T(8,128)(2,1)S(1)} %get-tuple-element.14), kind=kOutput, calls=%fused_computation.21 | convolution fusion | flops 705560576 | bytes 7438336 | tf_op jit(solution)/shard_map/dot_general | solution.py:230
  185.9 43.3 %reduce-scatter.6.cloned.1.call-done = bf16[32,7168]{1,0:T(8,128)(2,1)} async-done(((bf16[128,7168]{1,0:T(8,128)(2,1)}), bf16[32,7168]{1,0:T(8,128)(2,1)}) %reduce-scatter.6.cloned.1.call-update) | async-done | bytes 458768 | tf_op jit(solution)/shard_map/reduce_scatter | solution.py:235
  229.2 1.7 fusion.59
  230.9 2.7 fusion.57
  233.6 74.9 %shard_map.105 = (bf16[8,48,7168]{2,1,0:T(8,128)(2,1)S(1)}, bf16[4,32,7168]{2,1,0:T(8,128)(2,1)S(1)}) custom-call(bf16[32,7168]{1,0:T(8,128)(2,1)S(1)} %get-tuple-element.19.refs_0_, bf16[8,48,128]{2,1,0:T(8,128)(2,1)S(1)} %bitcast.142, f32[8,48,1]{2,1,0:T(8,128)S(1)} %reshape.87.refs_2_, bf16[32,7168]{1,0:T(8,128)(2,1)S(1)} %get-tuple-element.17.refs_3_), custom_call_target="tpu_custom_call" | custom-call | tf_op jit(solution)/shard_map/pallas_call | solution.py:165
  308.5 7.1 %fusion.9 = f32[8,48,608]{2,1,0:T(8,128)S(1)} fusion(bf16[8,48,7168]{2,1,0:T(8,128)(2,1)S(1)} %get-tuple-element.9, bf16[1,608,7168]{2,1,0:T(8,128)(2,1)} %param.13), kind=kOutput, calls=%fused_computation.11 | convolution fusion | flops 3347054592 | bytes 15155200 | tf_op jit(solution)/shard_map/scd,hd->sch/dot_general | solution.py:256
  315.6 10.8 %fusion.3 = f32[8,48,7168]{2,1,0:T(8,128)} fusion(bf16[1,2,608,7168]{3,2,1,0:T(8,128)(2,1)} %param.12, f32[8,48,608]{2,1,0:T(8,128)S(1)} %fusion.9, f32[8,48,2,608]{3,1,2,0:T(8,128)S(1)} %copy-done.3), kind=kOutput, calls=%fused_computation.5 | convolution fusion | flops 3349389312 | bytes 22528000 | tf_op jit(solution)/shard_map/sch,hd->scd/dot_general | solution.py:267
  326.4 11.4 %add_convert_fusion = bf16[8,48,7168]{2,1,0:T(8,128)(2,1)} fusion(f32[8,48,7168]{2,1,0:T(8,128)} %fusion.3, bf16[1,2,608,7168]{3,2,1,0:T(8,128)(2,1)} %param.12, f32[8,48,608]{2,1,0:T(8,128)S(1)} %fusion.9, f32[8,48,2,608]{3,1,2,0:T(8,128)S(1)} %copy-done.3), kind=kOutput, calls=%fused_computation.2 | convolution fusion | flops 3353960448 | bytes 27197440 | tf_op jit(solution)/shard_map/sch,hd->scd/dot_general | solution.py:268
  337.8 4.7 all-to-all-start.1
  342.4 0.3 reduce-scatter.8.cloned.1.call-start
  342.7 6.0 %fusion.85 = f32[128,608]{0,1:T(8,128)S(1)} fusion(bf16[128,7168]{1,0:T(8,128)(2,1)S(1)} %bitcast.139, bf16[608,7168]{1,0:T(8,128)(2,1)} %param.11), kind=kOutput, calls=%fused_computation.122 | convolution fusion | flops 1115684864 | bytes 10862592 | tf_op jit(solution)/shard_map/gd,hd->gh/dot_general | solution.py:248
  348.8 5.4 %fusion.5 = f32[128,7168]{1,0:T(8,128)S(1)} fusion(bf16[2,608,7168]{2,1,0:T(8,128)(2,1)} %param.10, f32[128,608]{0,1:T(8,128)S(1)} %fusion.85, f32[128,2,608]{0,2,1:T(8,128)S(1)} %fusion.84), kind=kOutput, calls=%fused_computation.7 | convolution fusion | flops 1116151808 | bytes 13008896 | tf_op jit(solution)/shard_map/dot_general | solution.py:253
  354.3 3.8 fusion.16
  358.1 47.5 %all-to-all-done.1 = bf16[8,48,7168]{2,1,0:T(8,128)(2,1)} async-done(((bf16[8,48,7168]{2,1,0:T(8,128)(2,1)}), bf16[8,48,7168]{2,1,0:T(8,128)(2,1)}, u32[]{:S(2)}, u32[]{:S(2)}) %all-to-all-start.1) | async-done | bytes 5505056 | tf_op jit(solution)/shard_map/all_to_all | solution.py:270
  405.6 6.0 %fusion.19 = bf16[128,7168]{1,0:T(8,128)(2,1)} fusion(f32[128,7168]{1,0:T(8,128)} %fusion.16, bf16[384,7168]{1,0:T(8,128)(2,1)} %bitcast.27, bf16[128,384]{1,0:T(8,128)(2,1)S(1)} %get-tuple-element.16), kind=kOutput, calls=%fused_computation.20 | convolution fusion | flops 706478080 | bytes 11108352 | tf_op jit(solution)/shard_map/dot_general | solution.py:272
  411.7 48.8 %reduce-scatter.8.cloned.1.call-done = bf16[32,7168]{1,0:T(8,128)(2,1)} async-done(((bf16[128,7168]{1,0:T(8,128)(2,1)}), bf16[32,7168]{1,0:T(8,128)(2,1)}) %reduce-scatter.8.cloned.1.call-update) | async-done | bytes 458768 | tf_op jit(solution)/shard_map/reduce_scatter | solution.py:273
  460.5 1.3 fusion.63
  461.8 2.1 fusion.47
  (34 shorter events, 1.3 us)
Async XLA Ops:
  101.7 1.3 copy-start.2
  112.8 68.0 %all-to-all-start = ((bf16[8,48,7168]{2,1,0:T(8,128)(2,1)}), bf16[8,48,7168]{2,1,0:T(8,128)(2,1)}, u32[]{:S(2)}, u32[]{:S(2)}) async-start(bf16[8,48,7168]{2,1,0:T(8,128)(2,1)} %convolution_convert_fusion), calls=%async_computation.1 | async-start | bytes 11010048 | tf_op jit(solution)/shard_map/all_to_all | solution.py:228
  117.5 68.4 %reduce-scatter.4.cloned.1.call-start = ((), (), s32[]{:S(2)}) async-start(), calls=%async_computation.5 | async-start | bytes 2293760 | tf_op jit(solution)/shard_map/reduce_scatter | solution.py:232
  132.4 96.8 %reduce-scatter.6.cloned.1.call-start = ((), (), s32[]{:S(2)}) async-start(), calls=%async_computation.6 | async-start | bytes 2293760 | tf_op jit(solution)/shard_map/reduce_scatter | solution.py:235
  180.8 48.4 %copy-start.1 = (bf16[32,7168]{1,0:T(8,128)(2,1)S(1)}, bf16[32,7168]{1,0:T(8,128)(2,1)}, u32[]{:S(2)}) copy-start(bf16[32,7168]{1,0:T(8,128)(2,1)} %param.17) | copy-start | bytes 1376260
  180.8 50.1 %copy-start = (bf16[32,7168]{1,0:T(8,128)(2,1)S(1)}, bf16[32,7168]{1,0:T(8,128)(2,1)}, u32[]{:S(2)}) copy-start(bf16[32,7168]{1,0:T(8,128)(2,1)} %param.9) | copy-start | bytes 1376260
  308.5 7.1 %copy-start.3 = (f32[8,48,2,608]{3,1,2,0:T(8,128)S(1)}, f32[8,48,2,608]{3,1,2,0:T(8,128)}, u32[]{:S(2)}) copy-start(f32[8,48,2,608]{3,1,2,0:T(8,128)} %copy-done.2) | copy-start | bytes 5603332
  337.8 67.9 %all-to-all-start.1 = ((bf16[8,48,7168]{2,1,0:T(8,128)(2,1)}), bf16[8,48,7168]{2,1,0:T(8,128)(2,1)}, u32[]{:S(2)}, u32[]{:S(2)}) async-start(bf16[8,48,7168]{2,1,0:T(8,128)(2,1)} %add_convert_fusion), calls=%async_computation.3 | async-start | bytes 11010048 | tf_op jit(solution)/shard_map/all_to_all | solution.py:270
  342.4 118.1 %reduce-scatter.8.cloned.1.call-start = ((), (), s32[]{:S(2)}) async-start(), calls=%async_computation.7 | async-start | bytes 2293760 | tf_op jit(solution)/shard_map/reduce_scatter | solution.py:273
  342.7 11.5 %slice-start = ((s8[17432576]{0:T(1024)(128)(4,1)}), s8[4194304]{0:T(1024)(128)(4,1)S(1)}, s32[]{:S(2)}) async-start(s8[17432576]{0:T(1024)(128)(4,1)} %bitcast.143), calls=%async_computation.8 | async-start | bytes 8388608
  342.7 11.5 %slice-start.1 = ((s8[17432576]{0:T(1024)(128)(4,1)}), s8[4194304]{0:T(1024)(128)(4,1)S(1)}, s32[]{:S(2)}) async-start(s8[17432576]{0:T(1024)(128)(4,1)} %bitcast.143), calls=%async_computation.9 | async-start | bytes 8388608
  342.7 11.5 %slice-start.2 = ((s8[17432576]{0:T(1024)(128)(4,1)}), s8[4194304]{0:T(1024)(128)(4,1)S(1)}, s32[]{:S(2)}) async-start(s8[17432576]{0:T(1024)(128)(4,1)} %bitcast.143), calls=%async_computation.10 | async-start | bytes 8388608
  348.8 5.5 %slice-start.3 = ((s8[17432576]{0:T(1024)(128)(4,1)}), s8[4194304]{0:T(1024)(128)(4,1)S(1)}, s32[]{:S(2)}) async-start(s8[17432576]{0:T(1024)(128)(4,1)} %bitcast.143), calls=%async_computation.11 | async-start | bytes 8388608
  348.8 5.5 %slice-start.4 = ((s8[17432576]{0:T(1024)(128)(4,1)}), s8[655360]{0:T(1024)(128)(4,1)S(1)}, s32[]{:S(2)}) async-start(s8[17432576]{0:T(1024)(128)(4,1)} %bitcast.143), calls=%async_computation.12 | async-start | bytes 1310720
Sparse Core Ops, SparseCore 0:
  132.5 45.3 reduce-scatter.3
  186.0 43.1 reduce-scatter.5
  411.8 48.6 reduce-scatter.7
